TPU v7x, 512 devices: a whole 4x8x8 slice. The times are simulated.
512 devices in a mesh: seq: 128 (over z, y, core), tp: 4 (over x).
Axes of the slice: x: 4, y: 8, z: 8, core: 2. Of those that a mesh axis runs over, the one named last changes fastest.
Arguments:
- state: bfloat16 [16384, 1024], P('seq', 'tp'), may hold values from -16 to 16
- cotangent: float32 [16384, 1024], P('seq', 'tp'), may hold values from -40 to 40
- norm_gain: float32 [1024], replicated, may hold values from 0.5 to 1.5
- w_query: bfloat16 [1024, 1024], P(None, 'tp'), may hold values from -8 to 8
- w_key: bfloat16 [1024, 1024], P(None, 'tp'), may hold values from -1 to 1
- w_value: bfloat16 [1024, 1024], P(None, 'tp'), may hold values from -0.1875 to 0.1875
- w_out: bfloat16 [1024, 1024], P('tp'), may hold values from -1.5 to 1.5
Outputs:
- adjoint: float32 [16384, 1024], P('seq', 'tp')
- residual: float32 [16384, 1024], P('seq', 'tp')
All inputs are finite; a program needn't handle non-finite values.
Results may differ from a plain program's by a relative error of at most 0.025.
The roundings to bfloat16 on the way count: a program that leaves them out, or rounds other values in their place, can miss the bound.
Values may be sent and summed in bfloat16 or wider, within the bound.
A program may use at most 64 MiB of HBM per device.

v0:
```python
import math
import jax
import jax.numpy as jnp
from jax import lax
from jax.sharding import Mesh
from jax.sharding import PartitionSpec as P

HD = 128
WIN = 1024
SSTEP = 4
SEQ = ("seq_0", "seq_1", "seq_2")
SEQ_TP = ("seq_0", "seq_1", "seq_2", "tp")
EPSILON = 1e-05


def from_everyone(array, axis):
    copies = jnp.broadcast_to(array, (lax.axis_size(axis), *array.shape))
    return lax.all_to_all(copies, axis, split_axis=0, concat_axis=0, tiled=True)


def in_order(parts, dim):
    dims = list(parts.shape[1:])
    dims[dim] *= parts.shape[0]
    return jnp.moveaxis(parts, 0, dim).reshape(dims)


def collect(array, axis, dim):
    parts = from_everyone(array, axis)
    return in_order(parts, dim)


def shifted(array, axis, by):
    length = lax.axis_size(axis)
    pairs = [(i, i + by) for i in range(length) if 0 <= i + by < length]
    return lax.ppermute(array, axis, pairs)


def cut_along(array, dim, length):
    before, after = (array.shape[:dim], array.shape[dim + 1 :])
    return jnp.moveaxis(array.reshape(*before, length, -1, *after), dim, 0)


def summed_on_arrival(array, axis, dim):
    parts = cut_along(array, dim, lax.axis_size(axis))
    arrived = lax.all_to_all(parts, axis, split_axis=0, concat_axis=0, tiled=True)
    return arrived.sum(axis=0)


def over_axes(array, axes):
    for axis in axes:
        array = lax.psum(array, axis)
    return array


def lower_solve(factor, values):
    result = []
    for index_i in range(values.shape[0]):
        running = values[index_i]
        for index_j in range(index_i):
            running = running - factor[index_i, index_j] * result[index_j]
        result.append(running / factor[index_i, index_i])
    return jnp.stack(result)


def upper_solve(factor, values):
    length_n = values.shape[0]
    result = [None] * length_n
    for index_i in range(length_n - 1, -1, -1):
        running = values[index_i]
        for index_j in range(index_i + 1, length_n):
            running = running - factor[index_j, index_i] * result[index_j]
        result[index_i] = running / factor[index_i, index_i]
    return jnp.stack(result)


def combine_coefficients(gram_matrix, right_side):
    factor = jnp.linalg.cholesky(gram_matrix)
    return upper_solve(factor, lower_solve(factor, right_side))


def on_device(state, cotangent, norm_gain, w_query, w_key, w_value, w_out):
    tok_rows = state.shape[0]
    cols_local = state.shape[1]
    attn_width = w_query.shape[1]
    heads_local = attn_width // HD
    half_span = WIN // 2
    edge_rows = min(tok_rows, half_span)
    reach_count = (half_span + tok_rows - 1) // tok_rows
    key_count = tok_rows + 2 * half_span
    total_rows = tok_rows * lax.axis_size(SEQ)
    first_row = lax.axis_index(SEQ) * tok_rows
    scale_factor = 1.0 / math.sqrt(HD)
    gain_local = lax.dynamic_slice_in_dim(
        norm_gain, lax.axis_index("tp") * cols_local, cols_local, 0
    )
    contract_last = (((1,), (1,)), ((), ()))
    full_state = collect(state, "tp", 1)
    state_full = full_state.astype(jnp.float32)
    inverse = lax.rsqrt(jnp.mean(state_full * state_full, axis=1, keepdims=True) + EPSILON)
    normed = (state_full * inverse * norm_gain[None, :]).astype(jnp.bfloat16)
    w_inputs = jnp.concatenate([w_query, w_key, w_value], axis=1)
    projected = jnp.dot(normed, w_inputs, preferred_element_type=jnp.float32).astype(jnp.bfloat16)
    queries = projected[:, :attn_width].reshape(tok_rows, heads_local, HD)
    key_vecs = projected[:, attn_width : 2 * attn_width].reshape(tok_rows, heads_local, HD)
    values = projected[:, 2 * attn_width :].reshape(tok_rows, heads_local, HD)
    left_parts = []
    for offset in range(reach_count, 0, -1):
        left_parts.append(shifted((key_vecs, values), SEQ, offset))
    right_parts = []
    for offset in range(1, reach_count + 1):
        right_parts.append(shifted((key_vecs, values), SEQ, -offset))
    keys_all = jnp.concatenate(
        [received[0] for received in left_parts]
        + [key_vecs]
        + [received[0] for received in right_parts],
        axis=0,
    )
    values_all = jnp.concatenate(
        [received[1] for received in left_parts]
        + [values]
        + [received[1] for received in right_parts],
        axis=0,
    )
    query_pos = first_row + jnp.arange(tok_rows, dtype=jnp.int32)
    key_pos = first_row - half_span + jnp.arange(key_count, dtype=jnp.int32)
    distance = jnp.abs(key_pos[None, :] - query_pos[:, None])
    valid = ((distance <= half_span) & (key_pos[None, :] >= 0) & (key_pos[None, :] < total_rows))[
        None
    ]
    scores = (
        jnp.einsum("rhe,khe->hrk", queries, keys_all, preferred_element_type=jnp.float32)
        * scale_factor
    )
    row_peak = jnp.max(jnp.where(valid, scores, -jnp.inf), axis=2, keepdims=True)
    raw_weights = jnp.where(valid, jnp.exp(scores - row_peak), 0.0)
    row_total = jnp.sum(raw_weights, axis=2, keepdims=True)
    attn_probs = raw_weights / row_total
    probs_low = attn_probs.astype(jnp.bfloat16)
    attended = jnp.einsum("hrk,khe->rhe", probs_low, values_all, preferred_element_type=jnp.float32)
    krylov = [cotangent]
    differences = []
    for index_n in range(SSTEP):
        whole_vec = collect(krylov[-1].astype(jnp.bfloat16), "tp", 1)
        grad_out = (
            lax.dot_general(whole_vec, w_out, contract_last, preferred_element_type=jnp.float32)
            .astype(jnp.bfloat16)
            .reshape(tok_rows, heads_local, HD)
        )
        row_corr = jnp.sum(grad_out.astype(jnp.float32) * attended, axis=2).T
        grad_prob = jnp.einsum(
            "rhe,khe->hrk", grad_out, values_all, preferred_element_type=jnp.float32
        )
        grad_score = (scale_factor * attn_probs * (grad_prob - row_corr[:, :, None])).astype(
            jnp.bfloat16
        )
        grad_query = jnp.einsum(
            "hrk,khe->rhe", grad_score, keys_all, preferred_element_type=jnp.float32
        ).astype(jnp.bfloat16)
        key_partial = jnp.einsum(
            "hrk,rhe->khe", grad_score, queries, preferred_element_type=jnp.float32
        )
        value_partial = jnp.einsum(
            "hrk,rhe->khe", probs_low, grad_out, preferred_element_type=jnp.float32
        )
        own_key = key_partial[half_span : half_span + tok_rows]
        own_value = value_partial[half_span : half_span + tok_rows]
        for cell_offset in range(1, reach_count + 1):
            lower_row = (reach_count - cell_offset) * edge_rows
            incoming = shifted(
                (
                    key_partial[lower_row : lower_row + edge_rows],
                    value_partial[lower_row : lower_row + edge_rows],
                ),
                SEQ,
                -cell_offset,
            )
            own_key = own_key.at[tok_rows - edge_rows :].add(incoming[0])
            own_value = own_value.at[tok_rows - edge_rows :].add(incoming[1])
        for cell_offset in range(1, reach_count + 1):
            upper_row = half_span + tok_rows + (cell_offset - 1) * edge_rows
            incoming = shifted(
                (
                    key_partial[upper_row : upper_row + edge_rows],
                    value_partial[upper_row : upper_row + edge_rows],
                ),
                SEQ,
                cell_offset,
            )
            own_key = own_key.at[:edge_rows].add(incoming[0])
            own_value = own_value.at[:edge_rows].add(incoming[1])
        grad_key = own_key.astype(jnp.bfloat16)
        grad_value = own_value.astype(jnp.bfloat16)
        stacked = jnp.concatenate(
            [
                grad_query.reshape(tok_rows, attn_width),
                grad_key.reshape(tok_rows, attn_width),
                grad_value.reshape(tok_rows, attn_width),
            ],
            axis=1,
        )
        partial_sum = lax.dot_general(
            stacked, w_inputs, contract_last, preferred_element_type=jnp.float32
        )
        summed = summed_on_arrival(partial_sum, "tp", 1)
        krylov.append(inverse * (gain_local[None, :] * summed))
        differences.append(krylov[index_n] - krylov[index_n + 1])
    diff_stack = jnp.stack(differences)
    local_gram = jnp.einsum("arc,brc->ab", diff_stack, diff_stack, precision=lax.Precision.HIGHEST)
    local_right = jnp.einsum("arc,rc->a", diff_stack, cotangent, precision=lax.Precision.HIGHEST)
    gram_matrix, right_side = (over_axes(local_gram, SEQ_TP), over_axes(local_right, SEQ_TP))
    coefficients = combine_coefficients(gram_matrix, right_side)
    adjoint = coefficients[0] * krylov[0]
    residual = cotangent - coefficients[0] * differences[0]
    for index_n in range(1, SSTEP):
        adjoint = adjoint + coefficients[index_n] * krylov[index_n]
        residual = residual - coefficients[index_n] * differences[index_n]
    return (adjoint, residual)


def solution(mesh):
    split = Mesh(mesh.devices.reshape(8, 8, 2, mesh.shape["tp"]), ("seq_0", "seq_1", "seq_2", "tp"))
    in_specs = (
        P(SEQ, "tp"),
        P(SEQ, "tp"),
        P(),
        P(None, "tp"),
        P(None, "tp"),
        P(None, "tp"),
        P("tp", None),
    )
    out_specs = (P(SEQ, "tp"), P(SEQ, "tp"))
    return jax.shard_map(
        on_device, mesh=split, in_specs=in_specs, out_specs=out_specs, check_vma=False
    )
```

profile of v0, /device:TPU:2, one launch (start us, length us, event | category | flops | bytes accessed | tf_op | source)
XLA Modules:
  0.0 517.0 jit_solution(13610098258207322927)
XLA Ops:
  2.5 9.3 %all-to-all-start = ((bf16[4,128,256]{1,2,0:T(8,128)(2,1)}), bf16[4,128,256]{1,2,0:T(8,128)(2,1)S(1)}, u32[]{:S(2)}, u32[]{:S(2)}) async-start(bf16[4,128,256]{1,2,0:T(8,128)(2,1)} %broadcast_in_dim.28), calls=%async_computation | async-start | bytes 524288 | tf_op jit(solution)/shard_map/all_to_all | solution.py:18
  41.4 7.5 %collective-permute-start.8 = (bf16[128,2,128]{2,0,1:T(8,128)(2,1)}, bf16[128,2,128]{2,0,1:T(8,128)(2,1)S(1)}, u32[]{:S(2)}, u32[]{:S(2)}) collective-permute-start(bf16[128,2,128]{2,0,1:T(8,128)(2,1)} %bitcast.190), channel_id=1, source_target_pairs={{0,16},{4,20},{8,24},{12,28},{16,32},{20,36},{24,40},{28,44},{32,4... | collective-permute-start | bytes 196616 | tf_op jit(solution)/shard_map/ppermute | solution.py:35
  91.2 6.4 %collective-permute-start.22 = (f32[128,2,128]{0,2,1:T(8,128)S(1)}, f32[128,2,128]{0,2,1:T(8,128)S(1)}, u32[]{:S(2)}, u32[]{:S(2)}) collective-permute-start(f32[128,2,128]{0,2,1:T(8,128)S(1)} %get-tuple-element.1346), channel_id=1, source_target_pairs={{0,12},{4,16},{8,20},{12,24},{16,28},{20,32},{24,36},{28,40},{32,4... | collective-permute-start | bytes 393224 | tf_op jit(solution)/shard_map/ppermute | solution.py:35
  97.6 6.2 %collective-permute-start.23 = (f32[128,2,128]{0,2,1:T(8,128)S(1)}, f32[128,2,128]{0,2,1:T(8,128)S(1)}, u32[]{:S(2)}, u32[]{:S(2)}) collective-permute-start(f32[128,2,128]{0,2,1:T(8,128)S(1)} %get-tuple-element.1345), channel_id=1, source_target_pairs={{0,16},{4,20},{8,24},{12,28},{16,32},{20,36},{24,40},{28,44},{32,4... | collective-permute-start | bytes 393224 | tf_op jit(solution)/shard_map/ppermute | solution.py:35
  117.6 7.2 %collective-permute-start.30 = (f32[128,2,128]{0,2,1:T(8,128)S(1)}, f32[128,2,128]{0,2,1:T(8,128)S(1)}, u32[]{:S(2)}, u32[]{:S(2)}) collective-permute-start(f32[128,2,128]{0,2,1:T(8,128)S(1)} %get-tuple-element.1354), channel_id=1, source_target_pairs={{0,12},{4,16},{8,20},{12,24},{16,28},{20,32},{24,36},{28,40},{32,4... | collective-permute-start | bytes 393224 | tf_op jit(solution)/shard_map/ppermute | solution.py:35
  124.8 6.6 %collective-permute-start.31 = (f32[128,2,128]{0,2,1:T(8,128)S(1)}, f32[128,2,128]{0,2,1:T(8,128)S(1)}, u32[]{:S(2)}, u32[]{:S(2)}) collective-permute-start(f32[128,2,128]{0,2,1:T(8,128)S(1)} %get-tuple-element.1353), channel_id=1, source_target_pairs={{0,16},{4,20},{8,24},{12,28},{16,32},{20,36},{24,40},{28,44},{32,4... | collective-permute-start | bytes 393224 | tf_op jit(solution)/shard_map/ppermute | solution.py:35
  143.1 5.5 %all-to-all-done.2 = f32[4,128,256]{2,1,0:T(8,128)} async-done(((f32[4,128,256]{2,1,0:T(8,128)}), f32[4,128,256]{2,1,0:T(8,128)}, u32[]{:S(2)}, u32[]{:S(2)}) %all-to-all-start.2) | async-done | bytes 524320 | tf_op jit(solution)/shard_map/all_to_all | solution.py:45
  153.8 9.1 %all_to_all.45 = bf16[4,128,256]{1,2,0:T(8,128)(2,1)S(1)} all-to-all(bf16[4,128,256]{1,2,0:T(8,128)(2,1)S(1)} %broadcast_in_dim.55), channel_id=1, replica_groups=mesh['seq_0'=8,'seq_1'=8,'seq_2'=2,'tp'=4] {'tp'}, dimensions={0} | all-to-all | bytes 524288 | tf_op jit(solution)/shard_map/all_to_all | solution.py:18
  175.6 8.1 %collective-permute-start.37 = (f32[128,2,128]{0,2,1:T(8,128)S(1)}, f32[128,2,128]{0,2,1:T(8,128)S(1)}, u32[]{:S(2)}, u32[]{:S(2)}) collective-permute-start(f32[128,2,128]{0,2,1:T(8,128)S(1)} %get-tuple-element.1331), channel_id=1, source_target_pairs={{0,8},{4,12},{8,16},{12,20},{16,24},{20,28},{24,32},{28,36},{32,40... | collective-permute-start | bytes 393224 | tf_op jit(solution)/shard_map/ppermute | solution.py:35
  183.9 5.4 %collective-permute-start.38 = (f32[128,2,128]{0,2,1:T(8,128)S(1)}, f32[128,2,128]{0,2,1:T(8,128)S(1)}, u32[]{:S(2)}, u32[]{:S(2)}) collective-permute-start(f32[128,2,128]{0,2,1:T(8,128)S(1)} %get-tuple-element.1330), channel_id=1, source_target_pairs={{0,12},{4,16},{8,20},{12,24},{16,28},{20,32},{24,36},{28,40},{32,4... | collective-permute-start | bytes 393224 | tf_op jit(solution)/shard_map/ppermute | solution.py:35
  189.3 6.1 %collective-permute-start.39 = (f32[128,2,128]{0,2,1:T(8,128)S(1)}, f32[128,2,128]{0,2,1:T(8,128)S(1)}, u32[]{:S(2)}, u32[]{:S(2)}) collective-permute-start(f32[128,2,128]{0,2,1:T(8,128)S(1)} %get-tuple-element.1329), channel_id=1, source_target_pairs={{0,16},{4,20},{8,24},{12,28},{16,32},{20,36},{24,40},{28,44},{32,4... | collective-permute-start | bytes 393224 | tf_op jit(solution)/shard_map/ppermute | solution.py:35
  209.3 7.0 %collective-permute-start.46 = (f32[128,2,128]{0,2,1:T(8,128)S(1)}, f32[128,2,128]{0,2,1:T(8,128)S(1)}, u32[]{:S(2)}, u32[]{:S(2)}) collective-permute-start(f32[128,2,128]{0,2,1:T(8,128)S(1)} %get-tuple-element.1338), channel_id=1, source_target_pairs={{0,12},{4,16},{8,20},{12,24},{16,28},{20,32},{24,36},{28,40},{32,4... | collective-permute-start | bytes 393224 | tf_op jit(solution)/shard_map/ppermute | solution.py:35
  216.4 6.4 %collective-permute-start.47 = (f32[128,2,128]{0,2,1:T(8,128)S(1)}, f32[128,2,128]{0,2,1:T(8,128)S(1)}, u32[]{:S(2)}, u32[]{:S(2)}) collective-permute-start(f32[128,2,128]{0,2,1:T(8,128)S(1)} %get-tuple-element.1337), channel_id=1, source_target_pairs={{0,16},{4,20},{8,24},{12,28},{16,32},{20,36},{24,40},{28,44},{32,4... | collective-permute-start | bytes 393224 | tf_op jit(solution)/shard_map/ppermute | solution.py:35
  227.3 12.2 %all_to_all.46 = f32[4,128,256]{2,1,0:T(8,128)} all-to-all(f32[4,128,256]{2,1,0:T(8,128)S(1)} %bitcast.198), channel_id=1, replica_groups=mesh['seq_0'=8,'seq_1'=8,'seq_2'=2,'tp'=4] {'tp'}, dimensions={0} | all-to-all | bytes 1048576 | tf_op jit(solution)/shard_map/all_to_all | solution.py:45
  243.9 9.1 %all_to_all.47 = bf16[4,128,256]{1,2,0:T(8,128)(2,1)S(1)} all-to-all(bf16[4,128,256]{1,2,0:T(8,128)(2,1)S(1)} %broadcast_in_dim.56), channel_id=1, replica_groups=mesh['seq_0'=8,'seq_1'=8,'seq_2'=2,'tp'=4] {'tp'}, dimensions={0} | all-to-all | bytes 524288 | tf_op jit(solution)/shard_map/all_to_all | solution.py:18
  265.8 7.9 %collective-permute-start.53 = (f32[128,2,128]{0,2,1:T(8,128)S(1)}, f32[128,2,128]{0,2,1:T(8,128)S(1)}, u32[]{:S(2)}, u32[]{:S(2)}) collective-permute-start(f32[128,2,128]{0,2,1:T(8,128)S(1)} %get-tuple-element.1315), channel_id=1, source_target_pairs={{0,8},{4,12},{8,16},{12,20},{16,24},{20,28},{24,32},{28,36},{32,40... | collective-permute-start | bytes 393224 | tf_op jit(solution)/shard_map/ppermute | solution.py:35
  273.8 5.4 %collective-permute-start.54 = (f32[128,2,128]{0,2,1:T(8,128)S(1)}, f32[128,2,128]{0,2,1:T(8,128)S(1)}, u32[]{:S(2)}, u32[]{:S(2)}) collective-permute-start(f32[128,2,128]{0,2,1:T(8,128)S(1)} %get-tuple-element.1314), channel_id=1, source_target_pairs={{0,12},{4,16},{8,20},{12,24},{16,28},{20,32},{24,36},{28,40},{32,4... | collective-permute-start | bytes 393224 | tf_op jit(solution)/shard_map/ppermute | solution.py:35
  279.3 6.1 %collective-permute-start.55 = (f32[128,2,128]{0,2,1:T(8,128)S(1)}, f32[128,2,128]{0,2,1:T(8,128)S(1)}, u32[]{:S(2)}, u32[]{:S(2)}) collective-permute-start(f32[128,2,128]{0,2,1:T(8,128)S(1)} %get-tuple-element.1313), channel_id=1, source_target_pairs={{0,16},{4,20},{8,24},{12,28},{16,32},{20,36},{24,40},{28,44},{32,4... | collective-permute-start | bytes 393224 | tf_op jit(solution)/shard_map/ppermute | solution.py:35
  299.2 7.1 %collective-permute-start.62 = (f32[128,2,128]{0,2,1:T(8,128)S(1)}, f32[128,2,128]{0,2,1:T(8,128)S(1)}, u32[]{:S(2)}, u32[]{:S(2)}) collective-permute-start(f32[128,2,128]{0,2,1:T(8,128)S(1)} %get-tuple-element.1322), channel_id=1, source_target_pairs={{0,12},{4,16},{8,20},{12,24},{16,28},{20,32},{24,36},{28,40},{32,4... | collective-permute-start | bytes 393224 | tf_op jit(solution)/shard_map/ppermute | solution.py:35
  306.3 6.6 %collective-permute-start.63 = (f32[128,2,128]{0,2,1:T(8,128)S(1)}, f32[128,2,128]{0,2,1:T(8,128)S(1)}, u32[]{:S(2)}, u32[]{:S(2)}) collective-permute-start(f32[128,2,128]{0,2,1:T(8,128)S(1)} %get-tuple-element.1321), channel_id=1, source_target_pairs={{0,16},{4,20},{8,24},{12,28},{16,32},{20,36},{24,40},{28,44},{32,4... | collective-permute-start | bytes 393224 | tf_op jit(solution)/shard_map/ppermute | solution.py:35
  316.9 12.3 %all_to_all.48 = f32[4,128,256]{2,1,0:T(8,128)} all-to-all(f32[4,128,256]{2,1,0:T(8,128)S(1)} %bitcast.199), channel_id=1, replica_groups=mesh['seq_0'=8,'seq_1'=8,'seq_2'=2,'tp'=4] {'tp'}, dimensions={0} | all-to-all | bytes 1048576 | tf_op jit(solution)/shard_map/all_to_all | solution.py:45
  333.7 9.1 %all_to_all.49 = bf16[4,128,256]{1,2,0:T(8,128)(2,1)S(1)} all-to-all(bf16[4,128,256]{1,2,0:T(8,128)(2,1)S(1)} %broadcast_in_dim.57), channel_id=1, replica_groups=mesh['seq_0'=8,'seq_1'=8,'seq_2'=2,'tp'=4] {'tp'}, dimensions={0} | all-to-all | bytes 524288 | tf_op jit(solution)/shard_map/all_to_all | solution.py:18
  355.5 8.1 %collective-permute-start.69 = (f32[128,2,128]{0,2,1:T(8,128)S(1)}, f32[128,2,128]{0,2,1:T(8,128)S(1)}, u32[]{:S(2)}, u32[]{:S(2)}) collective-permute-start(f32[128,2,128]{0,2,1:T(8,128)S(1)} %get-tuple-element.1299), channel_id=1, source_target_pairs={{0,8},{4,12},{8,16},{12,20},{16,24},{20,28},{24,32},{28,36},{32,40... | collective-permute-start | bytes 393224 | tf_op jit(solution)/shard_map/ppermute | solution.py:35
  363.8 5.4 %collective-permute-start.70 = (f32[128,2,128]{0,2,1:T(8,128)S(1)}, f32[128,2,128]{0,2,1:T(8,128)S(1)}, u32[]{:S(2)}, u32[]{:S(2)}) collective-permute-start(f32[128,2,128]{0,2,1:T(8,128)S(1)} %get-tuple-element.1298), channel_id=1, source_target_pairs={{0,12},{4,16},{8,20},{12,24},{16,28},{20,32},{24,36},{28,40},{32,4... | collective-permute-start | bytes 393224 | tf_op jit(solution)/shard_map/ppermute | solution.py:35
  369.2 6.1 %collective-permute-start.71 = (f32[128,2,128]{0,2,1:T(8,128)S(1)}, f32[128,2,128]{0,2,1:T(8,128)S(1)}, u32[]{:S(2)}, u32[]{:S(2)}) collective-permute-start(f32[128,2,128]{0,2,1:T(8,128)S(1)} %get-tuple-element.1297), channel_id=1, source_target_pairs={{0,16},{4,20},{8,24},{12,28},{16,32},{20,36},{24,40},{28,44},{32,4... | collective-permute-start | bytes 393224 | tf_op jit(solution)/shard_map/ppermute | solution.py:35
  384.0 5.2 collective-permute-start.77
  389.2 7.2 %collective-permute-start.78 = (f32[128,2,128]{0,2,1:T(8,128)S(1)}, f32[128,2,128]{0,2,1:T(8,128)S(1)}, u32[]{:S(2)}, u32[]{:S(2)}) collective-permute-start(f32[128,2,128]{0,2,1:T(8,128)S(1)} %get-tuple-element.1306), channel_id=1, source_target_pairs={{0,12},{4,16},{8,20},{12,24},{16,28},{20,32},{24,36},{28,40},{32,4... | collective-permute-start | bytes 393224 | tf_op jit(solution)/shard_map/ppermute | solution.py:35
  396.4 6.6 %collective-permute-start.79 = (f32[128,2,128]{0,2,1:T(8,128)S(1)}, f32[128,2,128]{0,2,1:T(8,128)S(1)}, u32[]{:S(2)}, u32[]{:S(2)}) collective-permute-start(f32[128,2,128]{0,2,1:T(8,128)S(1)} %get-tuple-element.1305), channel_id=1, source_target_pairs={{0,16},{4,20},{8,24},{12,28},{16,32},{20,36},{24,40},{28,44},{32,4... | collective-permute-start | bytes 393224 | tf_op jit(solution)/shard_map/ppermute | solution.py:35
  413.0 7.7 %all-to-all-done.8 = f32[4,128,256]{2,1,0:T(8,128)S(1)} async-done(((f32[4,128,256]{2,1,0:T(8,128)}), f32[4,128,256]{2,1,0:T(8,128)S(1)}, u32[]{:S(2)}, u32[]{:S(2)}) %all-to-all-start.8) | async-done | bytes 524320 | tf_op jit(solution)/shard_map/all_to_all | solution.py:45
  426.1 41.4 %all-reduce.1 = (f32[4]{0:T(128)S(1)}, f32[4,4]{0,1:T(4,128)S(1)}) all-reduce(f32[4]{0:T(128)S(1)} %convolution_bitcast_fusion.10, f32[4,4]{0,1:T(4,128)S(1)} %convolution_bitcast_fusion.9), channel_id=1, replica_groups=mesh['seq_0'=8,'seq_1'=8,'seq_2'=2,'tp'=4] {'seq_0'}, use_global_device_ids=true, to_apply=%region_11.12 | all-reduce | flops 20 | bytes 160 | tf_op jit(solution)/shard_map/psum | solution.py:51
  467.5 17.7 %all-reduce = (f32[4]{0:T(128)S(1)}, f32[4,4]{0,1:T(4,128)S(1)}) all-reduce(f32[4]{0:T(128)S(1)} %get-tuple-element.1290, f32[4,4]{0,1:T(4,128)S(1)} %get-tuple-element.1291), channel_id=1, replica_groups=mesh['seq_0'=8,'seq_1'=8,'seq_2'=2,'tp'=4] {'seq_1'}, use_global_device_ids=true, to_apply=%region_12.13 | all-reduce | flops 20 | bytes 160 | tf_op jit(solution)/shard_map/psum | solution.py:51
  487.7 9.2 %all-reduce.2 = (f32[4]{0:T(128)S(1)}, f32[4,4]{0,1:T(4,128)S(1)}) all-reduce(f32[4]{0:T(128)S(1)} %get-tuple-element.1294, f32[4,4]{0,1:T(4,128)S(1)} %get-tuple-element.1295), channel_id=1, replica_groups=mesh['seq_0'=8,'seq_1'=8,'seq_2'=2,'tp'=4] {'tp'}, use_global_device_ids=true, to_apply=%region_14.15 | all-reduce | flops 20 | bytes 160 | tf_op jit(solution)/shard_map/psum | solution.py:51
  (295 shorter events, 217.9 us)
Async XLA Ops:
  37.9 18.8 %collective-permute-start.6 = (bf16[128,2,128]{2,0,1:T(8,128)(2,1)S(1)}, bf16[128,2,128]{2,0,1:T(8,128)(2,1)S(1)}, u32[]{:S(2)}, u32[]{:S(2)}) collective-permute-start(bf16[128,2,128]{2,0,1:T(8,128)(2,1)S(1)} %bitcast.241), channel_id=1, source_target_pairs={{12,0},{16,4},{20,8},{24,12},{28,16},{32,20},{36,24},{40,28},{44,3... | collective-permute-start | bytes 196616 | tf_op jit(solution)/shard_map/ppermute | solution.py:35
  39.2 21.2 %collective-permute-start.7 = (bf16[128,2,128]{2,0,1:T(8,128)(2,1)S(1)}, bf16[128,2,128]{2,0,1:T(8,128)(2,1)S(1)}, u32[]{:S(2)}, u32[]{:S(2)}) collective-permute-start(bf16[128,2,128]{2,0,1:T(8,128)(2,1)S(1)} %bitcast.242), channel_id=1, source_target_pairs={{16,0},{20,4},{24,8},{28,12},{32,16},{36,20},{40,24},{44,28},{48,3... | collective-permute-start | bytes 196616 | tf_op jit(solution)/shard_map/ppermute | solution.py:35
  41.4 21.4 %collective-permute-start.8 = (bf16[128,2,128]{2,0,1:T(8,128)(2,1)}, bf16[128,2,128]{2,0,1:T(8,128)(2,1)S(1)}, u32[]{:S(2)}, u32[]{:S(2)}) collective-permute-start(bf16[128,2,128]{2,0,1:T(8,128)(2,1)} %bitcast.190), channel_id=1, source_target_pairs={{0,16},{4,20},{8,24},{12,28},{16,32},{20,36},{24,40},{28,44},{32,4... | collective-permute-start | bytes 196616 | tf_op jit(solution)/shard_map/ppermute | solution.py:35
  81.7 22.1 %collective-permute-start.19 = (f32[128,2,128]{0,2,1:T(8,128)S(1)}, f32[128,2,128]{0,2,1:T(8,128)S(1)}, u32[]{:S(2)}, u32[]{:S(2)}) collective-permute-start(f32[128,2,128]{0,2,1:T(8,128)S(1)} %get-tuple-element.1349), channel_id=1, source_target_pairs={{16,0},{20,4},{24,8},{28,12},{32,16},{36,20},{40,24},{44,28},{48,3... | collective-permute-start | bytes 393224 | tf_op jit(solution)/shard_map/ppermute | solution.py:35
  83.0 22.1 %collective-permute-start.20 = (f32[128,2,128]{0,2,1:T(8,128)S(1)}, f32[128,2,128]{0,2,1:T(8,128)S(1)}, u32[]{:S(2)}, u32[]{:S(2)}) collective-permute-start(f32[128,2,128]{0,2,1:T(8,128)S(1)} %get-tuple-element.1348), channel_id=1, source_target_pairs={{0,4},{4,8},{8,12},{12,16},{16,20},{20,24},{24,28},{28,32},{32,36}... | collective-permute-start | bytes 393224 | tf_op jit(solution)/shard_map/ppermute | solution.py:35
  86.0 20.3 %collective-permute-start.21 = (f32[128,2,128]{0,2,1:T(8,128)S(1)}, f32[128,2,128]{0,2,1:T(8,128)S(1)}, u32[]{:S(2)}, u32[]{:S(2)}) collective-permute-start(f32[128,2,128]{0,2,1:T(8,128)S(1)} %get-tuple-element.1347), channel_id=1, source_target_pairs={{0,8},{4,12},{8,16},{12,20},{16,24},{20,28},{24,32},{28,36},{32,40... | collective-permute-start | bytes 393224 | tf_op jit(solution)/shard_map/ppermute | solution.py:35
  106.4 18.4 %collective-permute-start.26 = (f32[128,2,128]{0,2,1:T(8,128)S(1)}, f32[128,2,128]{0,2,1:T(8,128)S(1)}, u32[]{:S(2)}, u32[]{:S(2)}) collective-permute-start(f32[128,2,128]{0,2,1:T(8,128)S(1)} %get-tuple-element.1358), channel_id=1, source_target_pairs={{12,0},{16,4},{20,8},{24,12},{28,16},{32,20},{36,24},{40,28},{44,3... | collective-permute-start | bytes 393224 | tf_op jit(solution)/shard_map/ppermute | solution.py:35
  108.1 23.4 %collective-permute-start.27 = (f32[128,2,128]{0,2,1:T(8,128)S(1)}, f32[128,2,128]{0,2,1:T(8,128)S(1)}, u32[]{:S(2)}, u32[]{:S(2)}) collective-permute-start(f32[128,2,128]{0,2,1:T(8,128)S(1)} %get-tuple-element.1357), channel_id=1, source_target_pairs={{16,0},{20,4},{24,8},{28,12},{32,16},{36,20},{40,24},{44,28},{48,3... | collective-permute-start | bytes 393224 | tf_op jit(solution)/shard_map/ppermute | solution.py:35
  109.4 22.1 %collective-permute-start.28 = (f32[128,2,128]{0,2,1:T(8,128)S(1)}, f32[128,2,128]{0,2,1:T(8,128)S(1)}, u32[]{:S(2)}, u32[]{:S(2)}) collective-permute-start(f32[128,2,128]{0,2,1:T(8,128)S(1)} %get-tuple-element.1356), channel_id=1, source_target_pairs={{0,4},{4,8},{8,12},{12,16},{16,20},{20,24},{24,28},{28,32},{32,36}... | collective-permute-start | bytes 393224 | tf_op jit(solution)/shard_map/ppermute | solution.py:35
  112.4 19.0 %collective-permute-start.29 = (f32[128,2,128]{0,2,1:T(8,128)S(1)}, f32[128,2,128]{0,2,1:T(8,128)S(1)}, u32[]{:S(2)}, u32[]{:S(2)}) collective-permute-start(f32[128,2,128]{0,2,1:T(8,128)S(1)} %get-tuple-element.1355), channel_id=1, source_target_pairs={{0,8},{4,12},{8,16},{12,20},{16,24},{20,28},{24,32},{28,36},{32,40... | collective-permute-start | bytes 393224 | tf_op jit(solution)/shard_map/ppermute | solution.py:35
  170.0 19.4 %collective-permute-start.34 = (f32[128,2,128]{0,2,1:T(8,128)S(1)}, f32[128,2,128]{0,2,1:T(8,128)S(1)}, u32[]{:S(2)}, u32[]{:S(2)}) collective-permute-start(f32[128,2,128]{0,2,1:T(8,128)S(1)} %get-tuple-element.1334), channel_id=1, source_target_pairs={{12,0},{16,4},{20,8},{24,12},{28,16},{32,20},{36,24},{40,28},{44,3... | collective-permute-start | bytes 393224 | tf_op jit(solution)/shard_map/ppermute | solution.py:35
  171.3 24.2 %collective-permute-start.35 = (f32[128,2,128]{0,2,1:T(8,128)S(1)}, f32[128,2,128]{0,2,1:T(8,128)S(1)}, u32[]{:S(2)}, u32[]{:S(2)}) collective-permute-start(f32[128,2,128]{0,2,1:T(8,128)S(1)} %get-tuple-element.1333), channel_id=1, source_target_pairs={{16,0},{20,4},{24,8},{28,12},{32,16},{36,20},{40,24},{44,28},{48,3... | collective-permute-start | bytes 393224 | tf_op jit(solution)/shard_map/ppermute | solution.py:35
  172.6 24.2 %collective-permute-start.36 = (f32[128,2,128]{0,2,1:T(8,128)S(1)}, f32[128,2,128]{0,2,1:T(8,128)S(1)}, u32[]{:S(2)}, u32[]{:S(2)}) collective-permute-start(f32[128,2,128]{0,2,1:T(8,128)S(1)} %get-tuple-element.1332), channel_id=1, source_target_pairs={{0,4},{4,8},{8,12},{12,16},{16,20},{20,24},{24,28},{28,32},{32,36}... | collective-permute-start | bytes 393224 | tf_op jit(solution)/shard_map/ppermute | solution.py:35
  175.6 22.5 %collective-permute-start.37 = (f32[128,2,128]{0,2,1:T(8,128)S(1)}, f32[128,2,128]{0,2,1:T(8,128)S(1)}, u32[]{:S(2)}, u32[]{:S(2)}) collective-permute-start(f32[128,2,128]{0,2,1:T(8,128)S(1)} %get-tuple-element.1331), channel_id=1, source_target_pairs={{0,8},{4,12},{8,16},{12,20},{16,24},{20,28},{24,32},{28,36},{32,40... | collective-permute-start | bytes 393224 | tf_op jit(solution)/shard_map/ppermute | solution.py:35
  199.8 23.1 %collective-permute-start.43 = (f32[128,2,128]{0,2,1:T(8,128)S(1)}, f32[128,2,128]{0,2,1:T(8,128)S(1)}, u32[]{:S(2)}, u32[]{:S(2)}) collective-permute-start(f32[128,2,128]{0,2,1:T(8,128)S(1)} %get-tuple-element.1341), channel_id=1, source_target_pairs={{16,0},{20,4},{24,8},{28,12},{32,16},{36,20},{40,24},{44,28},{48,3... | collective-permute-start | bytes 393224 | tf_op jit(solution)/shard_map/ppermute | solution.py:35
  201.1 21.8 %collective-permute-start.44 = (f32[128,2,128]{0,2,1:T(8,128)S(1)}, f32[128,2,128]{0,2,1:T(8,128)S(1)}, u32[]{:S(2)}, u32[]{:S(2)}) collective-permute-start(f32[128,2,128]{0,2,1:T(8,128)S(1)} %get-tuple-element.1340), channel_id=1, source_target_pairs={{0,4},{4,8},{8,12},{12,16},{16,20},{20,24},{24,28},{28,32},{32,36}... | collective-permute-start | bytes 393224 | tf_op jit(solution)/shard_map/ppermute | solution.py:35
  204.2 18.8 %collective-permute-start.45 = (f32[128,2,128]{0,2,1:T(8,128)S(1)}, f32[128,2,128]{0,2,1:T(8,128)S(1)}, u32[]{:S(2)}, u32[]{:S(2)}) collective-permute-start(f32[128,2,128]{0,2,1:T(8,128)S(1)} %get-tuple-element.1339), channel_id=1, source_target_pairs={{0,8},{4,12},{8,16},{12,20},{16,24},{20,28},{24,32},{28,36},{32,40... | collective-permute-start | bytes 393224 | tf_op jit(solution)/shard_map/ppermute | solution.py:35
  260.1 19.2 %collective-permute-start.50 = (f32[128,2,128]{0,2,1:T(8,128)S(1)}, f32[128,2,128]{0,2,1:T(8,128)S(1)}, u32[]{:S(2)}, u32[]{:S(2)}) collective-permute-start(f32[128,2,128]{0,2,1:T(8,128)S(1)} %get-tuple-element.1318), channel_id=1, source_target_pairs={{12,0},{16,4},{20,8},{24,12},{28,16},{32,20},{36,24},{40,28},{44,3... | collective-permute-start | bytes 393224 | tf_op jit(solution)/shard_map/ppermute | solution.py:35
  261.4 24.0 %collective-permute-start.51 = (f32[128,2,128]{0,2,1:T(8,128)S(1)}, f32[128,2,128]{0,2,1:T(8,128)S(1)}, u32[]{:S(2)}, u32[]{:S(2)}) collective-permute-start(f32[128,2,128]{0,2,1:T(8,128)S(1)} %get-tuple-element.1317), channel_id=1, source_target_pairs={{16,0},{20,4},{24,8},{28,12},{32,16},{36,20},{40,24},{44,28},{48,3... | collective-permute-start | bytes 393224 | tf_op jit(solution)/shard_map/ppermute | solution.py:35
  262.7 24.0 %collective-permute-start.52 = (f32[128,2,128]{0,2,1:T(8,128)S(1)}, f32[128,2,128]{0,2,1:T(8,128)S(1)}, u32[]{:S(2)}, u32[]{:S(2)}) collective-permute-start(f32[128,2,128]{0,2,1:T(8,128)S(1)} %get-tuple-element.1316), channel_id=1, source_target_pairs={{0,4},{4,8},{8,12},{12,16},{16,20},{20,24},{24,28},{28,32},{32,36}... | collective-permute-start | bytes 393224 | tf_op jit(solution)/shard_map/ppermute | solution.py:35
  265.8 22.3 %collective-permute-start.53 = (f32[128,2,128]{0,2,1:T(8,128)S(1)}, f32[128,2,128]{0,2,1:T(8,128)S(1)}, u32[]{:S(2)}, u32[]{:S(2)}) collective-permute-start(f32[128,2,128]{0,2,1:T(8,128)S(1)} %get-tuple-element.1315), channel_id=1, source_target_pairs={{0,8},{4,12},{8,16},{12,20},{16,24},{20,28},{24,32},{28,36},{32,40... | collective-permute-start | bytes 393224 | tf_op jit(solution)/shard_map/ppermute | solution.py:35
  289.7 23.3 %collective-permute-start.59 = (f32[128,2,128]{0,2,1:T(8,128)S(1)}, f32[128,2,128]{0,2,1:T(8,128)S(1)}, u32[]{:S(2)}, u32[]{:S(2)}) collective-permute-start(f32[128,2,128]{0,2,1:T(8,128)S(1)} %get-tuple-element.1325), channel_id=1, source_target_pairs={{16,0},{20,4},{24,8},{28,12},{32,16},{36,20},{40,24},{44,28},{48,3... | collective-permute-start | bytes 393224 | tf_op jit(solution)/shard_map/ppermute | solution.py:35
  291.0 22.0 %collective-permute-start.60 = (f32[128,2,128]{0,2,1:T(8,128)S(1)}, f32[128,2,128]{0,2,1:T(8,128)S(1)}, u32[]{:S(2)}, u32[]{:S(2)}) collective-permute-start(f32[128,2,128]{0,2,1:T(8,128)S(1)} %get-tuple-element.1324), channel_id=1, source_target_pairs={{0,4},{4,8},{8,12},{12,16},{16,20},{20,24},{24,28},{28,32},{32,36}... | collective-permute-start | bytes 393224 | tf_op jit(solution)/shard_map/ppermute | solution.py:35
  294.1 18.9 %collective-permute-start.61 = (f32[128,2,128]{0,2,1:T(8,128)S(1)}, f32[128,2,128]{0,2,1:T(8,128)S(1)}, u32[]{:S(2)}, u32[]{:S(2)}) collective-permute-start(f32[128,2,128]{0,2,1:T(8,128)S(1)} %get-tuple-element.1323), channel_id=1, source_target_pairs={{0,8},{4,12},{8,16},{12,20},{16,24},{20,28},{24,32},{28,36},{32,40... | collective-permute-start | bytes 393224 | tf_op jit(solution)/shard_map/ppermute | solution.py:35
  349.8 19.3 %collective-permute-start.66 = (f32[128,2,128]{0,2,1:T(8,128)S(1)}, f32[128,2,128]{0,2,1:T(8,128)S(1)}, u32[]{:S(2)}, u32[]{:S(2)}) collective-permute-start(f32[128,2,128]{0,2,1:T(8,128)S(1)} %get-tuple-element.1302), channel_id=1, source_target_pairs={{12,0},{16,4},{20,8},{24,12},{28,16},{32,20},{36,24},{40,28},{44,3... | collective-permute-start | bytes 393224 | tf_op jit(solution)/shard_map/ppermute | solution.py:35
  351.1 24.2 %collective-permute-start.67 = (f32[128,2,128]{0,2,1:T(8,128)S(1)}, f32[128,2,128]{0,2,1:T(8,128)S(1)}, u32[]{:S(2)}, u32[]{:S(2)}) collective-permute-start(f32[128,2,128]{0,2,1:T(8,128)S(1)} %get-tuple-element.1301), channel_id=1, source_target_pairs={{16,0},{20,4},{24,8},{28,12},{32,16},{36,20},{40,24},{44,28},{48,3... | collective-permute-start | bytes 393224 | tf_op jit(solution)/shard_map/ppermute | solution.py:35
  352.4 24.2 %collective-permute-start.68 = (f32[128,2,128]{0,2,1:T(8,128)S(1)}, f32[128,2,128]{0,2,1:T(8,128)S(1)}, u32[]{:S(2)}, u32[]{:S(2)}) collective-permute-start(f32[128,2,128]{0,2,1:T(8,128)S(1)} %get-tuple-element.1300), channel_id=1, source_target_pairs={{0,4},{4,8},{8,12},{12,16},{16,20},{20,24},{24,28},{28,32},{32,36}... | collective-permute-start | bytes 393224 | tf_op jit(solution)/shard_map/ppermute | solution.py:35
  355.5 22.5 %collective-permute-start.69 = (f32[128,2,128]{0,2,1:T(8,128)S(1)}, f32[128,2,128]{0,2,1:T(8,128)S(1)}, u32[]{:S(2)}, u32[]{:S(2)}) collective-permute-start(f32[128,2,128]{0,2,1:T(8,128)S(1)} %get-tuple-element.1299), channel_id=1, source_target_pairs={{0,8},{4,12},{8,16},{12,20},{16,24},{20,28},{24,32},{28,36},{32,40... | collective-permute-start | bytes 393224 | tf_op jit(solution)/shard_map/ppermute | solution.py:35
  378.0 18.4 %collective-permute-start.74 = (f32[128,2,128]{0,2,1:T(8,128)S(1)}, f32[128,2,128]{0,2,1:T(8,128)S(1)}, u32[]{:S(2)}, u32[]{:S(2)}) collective-permute-start(f32[128,2,128]{0,2,1:T(8,128)S(1)} %get-tuple-element.1310), channel_id=1, source_target_pairs={{12,0},{16,4},{20,8},{24,12},{28,16},{32,20},{36,24},{40,28},{44,3... | collective-permute-start | bytes 393224 | tf_op jit(solution)/shard_map/ppermute | solution.py:35
  379.6 23.4 %collective-permute-start.75 = (f32[128,2,128]{0,2,1:T(8,128)S(1)}, f32[128,2,128]{0,2,1:T(8,128)S(1)}, u32[]{:S(2)}, u32[]{:S(2)}) collective-permute-start(f32[128,2,128]{0,2,1:T(8,128)S(1)} %get-tuple-element.1309), channel_id=1, source_target_pairs={{16,0},{20,4},{24,8},{28,12},{32,16},{36,20},{40,24},{44,28},{48,3... | collective-permute-start | bytes 393224 | tf_op jit(solution)/shard_map/ppermute | solution.py:35
  381.0 22.1 %collective-permute-start.76 = (f32[128,2,128]{0,2,1:T(8,128)S(1)}, f32[128,2,128]{0,2,1:T(8,128)S(1)}, u32[]{:S(2)}, u32[]{:S(2)}) collective-permute-start(f32[128,2,128]{0,2,1:T(8,128)S(1)} %get-tuple-element.1308), channel_id=1, source_target_pairs={{0,4},{4,8},{8,12},{12,16},{16,20},{20,24},{24,28},{28,32},{32,36}... | collective-permute-start | bytes 393224 | tf_op jit(solution)/shard_map/ppermute | solution.py:35
  384.0 19.1 %collective-permute-start.77 = (f32[128,2,128]{0,2,1:T(8,128)S(1)}, f32[128,2,128]{0,2,1:T(8,128)S(1)}, u32[]{:S(2)}, u32[]{:S(2)}) collective-permute-start(f32[128,2,128]{0,2,1:T(8,128)S(1)} %get-tuple-element.1307), channel_id=1, source_target_pairs={{0,8},{4,12},{8,16},{12,20},{16,24},{20,28},{24,32},{28,36},{32,40... | collective-permute-start | bytes 393224 | tf_op jit(solution)/shard_map/ppermute | solution.py:35
  (65 other events, 872.4 us)
where the time goes:
time: 521 us; the launch traced here: 517 us
  starting transfers between devices  281 us (54%)
  blocking collectives  122 us (23%)
  waiting for transfers between devices  39.2 us (8%)
  local copies, waits for them, and re-layouts  21.6 us (4%)
  matrix products  21.5 us (4%)
  between operations  17.8 us (3%)
  other arithmetic  13.2 us (3%)
    ppermute x80, starting transfers between devices, shifted(): return lax.ppermute(array, axis, pairs)  257 us
    psum x4, blocking collectives, over_axes(): array = lax.psum(array, axis)  70.7 us
    all_to_all x3, blocking collectives, from_everyone(): return lax.all_to_all(copies, axis, split_axis=0, concat_axis=0, tiled=True)  27.2 us
    all_to_all x2, blocking collectives, summed_on_arrival(): lax.all_to_all(parts, axis, split_axis=0, concat_axis=0, tiled=True)  24.5 us
    ppermute x80, waiting for transfers between devices, shifted(): return lax.ppermute(array, axis, pairs)  22.4 us
    all_to_all x2, starting transfers between devices, from_everyone(): return lax.all_to_all(copies, axis, split_axis=0, concat_axis=0, tiled=True)  14.1 us
    all_to_all x2, waiting for transfers between devices, summed_on_arrival(): lax.all_to_all(parts, axis, split_axis=0, concat_axis=0, tiled=True)  13.2 us
  transfers between devices with their start and end apart: 84, of which 10 were waited for; matrix products, arithmetic and copies ran while one was open for 2% of the time, Pallas kernels for 0%

commit v1 on v0

--- a/solution.py
+++ b/solution.py
@@ -48,7 +48,7 @@
 
 def over_axes(array, axes):
     for axis in axes:
-        array = lax.psum(array, axis)
+        array = jnp.sum(lax.all_gather(array, axis), axis=0)
     return array
 
 

time: 521 us -> 577 us (1.11)
  the two profiles are of different devices: /device:TPU:2 before, /device:TPU:64 now
where the time goes in v1:
time: 577 us; the launch traced here: 573 us
  starting transfers between devices  266 us (46%)
  blocking collectives  167 us (29%)
  waiting for transfers between devices  55.3 us (10%)
  local copies, waits for them, and re-layouts  28 us (5%)
  matrix products  21.7 us (4%)
  between operations  20.2 us (4%)
  other arithmetic  14.5 us (3%)
    ppermute x80, starting transfers between devices, shifted(): return lax.ppermute(array, axis, pairs)  250 us
    all_gather x4, blocking collectives, over_axes(): array = jnp.sum(lax.all_gather(array, axis), axis=0)  71.6 us
    unnamed x4, blocking collectives  43.3 us
    ppermute x80, waiting for transfers between devices, shifted(): return lax.ppermute(array, axis, pairs)  42.3 us
    all_to_all x3, blocking collectives, from_everyone(): return lax.all_to_all(copies, axis, split_axis=0, concat_axis=0, tiled=True)  27.2 us
    all_to_all x2, blocking collectives, summed_on_arrival(): lax.all_to_all(parts, axis, split_axis=0, concat_axis=0, tiled=True)  25 us
    unnamed x62, local copies, waits for them, and re-layouts  12.1 us
  transfers between devices with their start and end apart: 84, of which 13 were waited for; matrix products, arithmetic and copies ran while one was open for 3% of the time, Pallas kernels for 0%

profile of v1, /device:TPU:64, one launch (start us, length us, event | category | flops | bytes accessed | tf_op | source)
XLA Modules:
  0.0 572.9 jit_solution(3803015608392209092)
XLA Ops:
  18.4 4.5 collective-permute-start
  33.0 5.0 collective-permute-start.4
  54.3 4.7 collective-permute-start.10
  61.1 5.7 collective-permute-start.12
  75.9 5.2 collective-permute-done.15
  107.6 5.2 collective-permute-start.24
  129.8 4.6 collective-permute-start.31
  137.7 5.5 collective-permute-done.31
  144.8 4.8 all-to-all-start.2
  151.3 7.7 %all-to-all-done.2 = f32[4,128,256]{2,1,0:T(8,128)} async-done(((f32[4,128,256]{2,1,0:T(8,128)}), f32[4,128,256]{2,1,0:T(8,128)}, u32[]{:S(2)}, u32[]{:S(2)}) %all-to-all-start.2) | async-done | bytes 524320 | tf_op jit(solution)/shard_map/all_to_all | solution.py:45
  164.1 9.1 %all_to_all.45 = bf16[4,128,256]{1,2,0:T(8,128)(2,1)S(1)} all-to-all(bf16[4,128,256]{1,2,0:T(8,128)(2,1)S(1)} %broadcast_in_dim.55), channel_id=1, replica_groups=mesh['seq_0'=8,'seq_1'=8,'seq_2'=2,'tp'=4] {'tp'}, dimensions={0} | all-to-all | bytes 524288 | tf_op jit(solution)/shard_map/all_to_all | solution.py:18
  192.0 4.6 collective-permute-start.38
  196.6 5.5 collective-permute-start.39
  218.6 4.5 collective-permute-start.46
  230.5 5.9 %collective-permute-done.47 = f32[128,2,128]{0,2,1:T(8,128)S(1)} collective-permute-done((f32[128,2,128]{0,2,1:T(8,128)S(1)}, f32[128,2,128]{0,2,1:T(8,128)S(1)}, u32[]{:S(2)}, u32[]{:S(2)}) %collective-permute-start.47) | collective-permute-done | bytes 131104 | tf_op jit(solution)/shard_map/ppermute | solution.py:35
  237.1 12.4 %all_to_all.48 = f32[4,128,256]{2,1,0:T(8,128)} all-to-all(f32[4,128,256]{2,1,0:T(8,128)S(1)} %bitcast.206), channel_id=1, replica_groups=mesh['seq_0'=8,'seq_1'=8,'seq_2'=2,'tp'=4] {'tp'}, dimensions={0} | all-to-all | bytes 1048576 | tf_op jit(solution)/shard_map/all_to_all | solution.py:45
  254.0 9.1 %all_to_all.46 = bf16[4,128,256]{1,2,0:T(8,128)(2,1)S(1)} all-to-all(bf16[4,128,256]{1,2,0:T(8,128)(2,1)S(1)} %broadcast_in_dim.56), channel_id=1, replica_groups=mesh['seq_0'=8,'seq_1'=8,'seq_2'=2,'tp'=4] {'tp'}, dimensions={0} | all-to-all | bytes 524288 | tf_op jit(solution)/shard_map/all_to_all | solution.py:18
  281.8 4.6 collective-permute-start.54
  286.5 5.5 collective-permute-start.55
  312.9 4.4 collective-permute-start.63
  320.5 5.8 %collective-permute-done.63 = f32[128,2,128]{0,2,1:T(8,128)S(1)} collective-permute-done((f32[128,2,128]{0,2,1:T(8,128)S(1)}, f32[128,2,128]{0,2,1:T(8,128)S(1)}, u32[]{:S(2)}, u32[]{:S(2)}) %collective-permute-start.63) | collective-permute-done | bytes 131104 | tf_op jit(solution)/shard_map/ppermute | solution.py:35
  327.1 12.5 %all_to_all.49 = f32[4,128,256]{2,1,0:T(8,128)} all-to-all(f32[4,128,256]{2,1,0:T(8,128)S(1)} %bitcast.207), channel_id=1, replica_groups=mesh['seq_0'=8,'seq_1'=8,'seq_2'=2,'tp'=4] {'tp'}, dimensions={0} | all-to-all | bytes 1048576 | tf_op jit(solution)/shard_map/all_to_all | solution.py:45
  344.1 9.1 %all_to_all.47 = bf16[4,128,256]{1,2,0:T(8,128)(2,1)S(1)} all-to-all(bf16[4,128,256]{1,2,0:T(8,128)(2,1)S(1)} %broadcast_in_dim.57), channel_id=1, replica_groups=mesh['seq_0'=8,'seq_1'=8,'seq_2'=2,'tp'=4] {'tp'}, dimensions={0} | all-to-all | bytes 524288 | tf_op jit(solution)/shard_map/all_to_all | solution.py:18
  371.8 4.6 collective-permute-start.70
  376.5 5.5 collective-permute-start.71
  410.5 5.9 %collective-permute-done.79 = f32[128,2,128]{0,2,1:T(8,128)S(1)} collective-permute-done((f32[128,2,128]{0,2,1:T(8,128)S(1)}, f32[128,2,128]{0,2,1:T(8,128)S(1)}, u32[]{:S(2)}, u32[]{:S(2)}) %collective-permute-start.79) | collective-permute-done | bytes 131104 | tf_op jit(solution)/shard_map/ppermute | solution.py:35
  434.1 38.4 %all-gather.8 = f32[8,4,4]{2,1,0:T(4,128)S(1)} all-gather(f32[1,4,4]{2,1,0:T(4,128)S(1)} %convolution_bitcast_fusion.9), channel_id=6, replica_groups=mesh['seq_0'=8,'seq_1'=8,'seq_2'=2,'tp'=4] {'seq_0'}, dimensions={0}, use_global_device_ids=true | all-gather | bytes 576 | tf_op jit(solution)/shard_map/all_gather | solution.py:51
  472.5 20.8 %all-gather.9 = f32[8,4,4]{2,1,0:T(4,128)S(1)} all-gather(f32[1,4,4]{2,1,0:T(4,128)S(1)} %bitcast.251), channel_id=7, replica_groups=mesh['seq_0'=8,'seq_1'=8,'seq_2'=2,'tp'=4] {'seq_1'}, dimensions={0}, use_global_device_ids=true | all-gather | bytes 576 | tf_op jit(solution)/shard_map/all_gather | solution.py:51
  495.2 10.6 %all-gather.11 = f32[4,4,4]{2,1,0:T(4,128)S(1)} all-gather(f32[1,4,4]{2,1,0:T(4,128)S(1)} %bitcast.253), channel_id=9, replica_groups=mesh['seq_0'=8,'seq_1'=8,'seq_2'=2,'tp'=4] {'tp'}, dimensions={0}, use_global_device_ids=true | all-gather | bytes 320 | tf_op jit(solution)/shard_map/all_gather | solution.py:51
  510.3 16.1 %all-reduce = f32[32]{0:T(128)S(1)} all-reduce(f32[32]{0:T(128)S(1)} %dynamic-update-slice.131), channel_id=2, replica_groups=mesh['seq_0'=8,'seq_1'=8,'seq_2'=2,'tp'=4] {'seq_0'}, use_global_device_ids=true, to_apply=%add | all-reduce | flops 32 | bytes 256
  526.7 15.3 %all-reduce.1 = f32[32]{0:T(128)S(1)} all-reduce(f32[32]{0:T(128)S(1)} %dynamic-update-slice.132), channel_id=3, replica_groups=mesh['seq_0'=8,'seq_1'=8,'seq_2'=2,'tp'=4] {'seq_1'}, use_global_device_ids=true, to_apply=%add.1 | all-reduce | flops 32 | bytes 256
  545.8 9.5 %all-reduce.3 = f32[16]{0:T(128)S(1)} all-reduce(f32[16]{0:T(128)S(1)} %dynamic-update-slice.134), channel_id=5, replica_groups=mesh['seq_0'=8,'seq_1'=8,'seq_2'=2,'tp'=4] {'tp'}, use_global_device_ids=true, to_apply=%add.3 | all-reduce | flops 16 | bytes 128
  (323 shorter events, 280.0 us)
Async XLA Ops:
  14.2 23.8 %all-to-all-start.1 = ((bf16[4,128,256]{1,2,0:T(8,128)(2,1)}), bf16[4,128,256]{1,2,0:T(8,128)(2,1)S(1)}, u32[]{:S(2)}, u32[]{:S(2)}) async-start(bf16[4,128,256]{1,2,0:T(8,128)(2,1)} %broadcast_in_dim.54), calls=%async_computation.1 | async-start | bytes 524288 | tf_op jit(solution)/shard_map/all_to_all | solution.py:18
  18.4 20.8 %collective-permute-start = (bf16[128,2,128]{2,0,1:T(8,128)(2,1)S(1)}, bf16[128,2,128]{2,0,1:T(8,128)(2,1)S(1)}, u32[]{:S(2)}, u32[]{:S(2)}) collective-permute-start(bf16[128,2,128]{2,0,1:T(8,128)(2,1)S(1)} %bitcast.243), channel_id=1, source_target_pairs={{0,16},{4,20},{8,24},{12,28},{16,32},{20,36},{24,40},{28,44},{32,4... | collective-permute-start | bytes 196616 | tf_op jit(solution)/shard_map/ppermute | solution.py:35
  22.9 18.6 %collective-permute-start.1 = (bf16[128,2,128]{2,0,1:T(8,128)(2,1)S(1)}, bf16[128,2,128]{2,0,1:T(8,128)(2,1)S(1)}, u32[]{:S(2)}, u32[]{:S(2)}) collective-permute-start(bf16[128,2,128]{2,0,1:T(8,128)(2,1)S(1)} %bitcast.244), channel_id=1, source_target_pairs={{0,12},{4,16},{8,20},{12,24},{16,28},{20,32},{24,36},{28,40},{32,4... | collective-permute-start | bytes 196616 | tf_op jit(solution)/shard_map/ppermute | solution.py:35
  24.8 18.6 %collective-permute-start.2 = (bf16[128,2,128]{2,0,1:T(8,128)(2,1)S(1)}, bf16[128,2,128]{2,0,1:T(8,128)(2,1)}, u32[]{:S(2)}, u32[]{:S(2)}) collective-permute-start(bf16[128,2,128]{2,0,1:T(8,128)(2,1)S(1)} %bitcast.245), channel_id=1, source_target_pairs={{0,8},{4,12},{8,16},{12,20},{16,24},{20,28},{24,32},{28,36},{32,40... | collective-permute-start | bytes 196616 | tf_op jit(solution)/shard_map/ppermute | solution.py:35
  28.9 17.9 %collective-permute-start.3 = (bf16[128,2,128]{2,0,1:T(8,128)(2,1)S(1)}, bf16[128,2,128]{2,0,1:T(8,128)(2,1)S(1)}, u32[]{:S(2)}, u32[]{:S(2)}) collective-permute-start(bf16[128,2,128]{2,0,1:T(8,128)(2,1)S(1)} %bitcast.246), channel_id=1, source_target_pairs={{0,4},{4,8},{8,12},{12,16},{16,20},{20,24},{24,28},{28,32},{32,36}... | collective-permute-start | bytes 196616 | tf_op jit(solution)/shard_map/ppermute | solution.py:35
  33.0 18.2 %collective-permute-start.4 = (bf16[128,2,128]{2,0,1:T(8,128)(2,1)S(1)}, bf16[128,2,128]{2,0,1:T(8,128)(2,1)S(1)}, u32[]{:S(2)}, u32[]{:S(2)}) collective-permute-start(bf16[128,2,128]{2,0,1:T(8,128)(2,1)S(1)} %bitcast.247), channel_id=1, source_target_pairs={{4,0},{8,4},{12,8},{16,12},{20,16},{24,20},{28,24},{32,28},{36,32}... | collective-permute-start | bytes 196616 | tf_op jit(solution)/shard_map/ppermute | solution.py:35
  41.5 17.5 %collective-permute-start.6 = (bf16[128,2,128]{2,0,1:T(8,128)(2,1)S(1)}, bf16[128,2,128]{2,0,1:T(8,128)(2,1)S(1)}, u32[]{:S(2)}, u32[]{:S(2)}) collective-permute-start(bf16[128,2,128]{2,0,1:T(8,128)(2,1)S(1)} %bitcast.249), channel_id=1, source_target_pairs={{12,0},{16,4},{20,8},{24,12},{28,16},{32,20},{36,24},{40,28},{44,3... | collective-permute-start | bytes 196616 | tf_op jit(solution)/shard_map/ppermute | solution.py:35
  43.5 17.6 %collective-permute-start.7 = (bf16[128,2,128]{2,0,1:T(8,128)(2,1)S(1)}, bf16[128,2,128]{2,0,1:T(8,128)(2,1)S(1)}, u32[]{:S(2)}, u32[]{:S(2)}) collective-permute-start(bf16[128,2,128]{2,0,1:T(8,128)(2,1)S(1)} %bitcast.250), channel_id=1, source_target_pairs={{16,0},{20,4},{24,8},{28,12},{32,16},{36,20},{40,24},{44,28},{48,3... | collective-permute-start | bytes 196616 | tf_op jit(solution)/shard_map/ppermute | solution.py:35
  46.7 21.1 %collective-permute-start.8 = (bf16[128,2,128]{2,0,1:T(8,128)(2,1)}, bf16[128,2,128]{2,0,1:T(8,128)(2,1)S(1)}, u32[]{:S(2)}, u32[]{:S(2)}) collective-permute-start(bf16[128,2,128]{2,0,1:T(8,128)(2,1)} %bitcast.198), channel_id=1, source_target_pairs={{0,16},{4,20},{8,24},{12,28},{16,32},{20,36},{24,40},{28,44},{32,4... | collective-permute-start | bytes 196616 | tf_op jit(solution)/shard_map/ppermute | solution.py:35
  51.2 18.7 %collective-permute-start.9 = (bf16[128,2,128]{2,0,1:T(8,128)(2,1)}, bf16[128,2,128]{2,0,1:T(8,128)(2,1)S(1)}, u32[]{:S(2)}, u32[]{:S(2)}) collective-permute-start(bf16[128,2,128]{2,0,1:T(8,128)(2,1)} %bitcast.198), channel_id=1, source_target_pairs={{0,12},{4,16},{8,20},{12,24},{16,28},{20,32},{24,36},{28,40},{32,4... | collective-permute-start | bytes 196616 | tf_op jit(solution)/shard_map/ppermute | solution.py:35
  54.3 17.5 %collective-permute-start.10 = (bf16[128,2,128]{2,0,1:T(8,128)(2,1)}, bf16[128,2,128]{2,0,1:T(8,128)(2,1)S(1)}, u32[]{:S(2)}, u32[]{:S(2)}) collective-permute-start(bf16[128,2,128]{2,0,1:T(8,128)(2,1)} %bitcast.198), channel_id=1, source_target_pairs={{0,8},{4,12},{8,16},{12,20},{16,24},{20,28},{24,32},{28,36},{32,40... | collective-permute-start | bytes 196616 | tf_op jit(solution)/shard_map/ppermute | solution.py:35
  93.2 19.6 %collective-permute-start.20 = (f32[128,2,128]{0,2,1:T(8,128)S(1)}, f32[128,2,128]{0,2,1:T(8,128)S(1)}, u32[]{:S(2)}, u32[]{:S(2)}) collective-permute-start(f32[128,2,128]{0,2,1:T(8,128)S(1)} %get-tuple-element.1340), channel_id=1, source_target_pairs={{0,4},{4,8},{8,12},{12,16},{16,20},{20,24},{24,28},{28,32},{32,36}... | collective-permute-start | bytes 393224 | tf_op jit(solution)/shard_map/ppermute | solution.py:35
  95.6 19.6 %collective-permute-start.21 = (f32[128,2,128]{0,2,1:T(8,128)S(1)}, f32[128,2,128]{0,2,1:T(8,128)S(1)}, u32[]{:S(2)}, u32[]{:S(2)}) collective-permute-start(f32[128,2,128]{0,2,1:T(8,128)S(1)} %get-tuple-element.1339), channel_id=1, source_target_pairs={{0,8},{4,12},{8,16},{12,20},{16,24},{20,28},{24,32},{28,36},{32,40... | collective-permute-start | bytes 393224 | tf_op jit(solution)/shard_map/ppermute | solution.py:35
  99.3 18.3 %collective-permute-start.22 = (f32[128,2,128]{0,2,1:T(8,128)S(1)}, f32[128,2,128]{0,2,1:T(8,128)S(1)}, u32[]{:S(2)}, u32[]{:S(2)}) collective-permute-start(f32[128,2,128]{0,2,1:T(8,128)S(1)} %get-tuple-element.1338), channel_id=1, source_target_pairs={{0,12},{4,16},{8,20},{12,24},{16,28},{20,32},{24,36},{28,40},{32,4... | collective-permute-start | bytes 393224 | tf_op jit(solution)/shard_map/ppermute | solution.py:35
  103.7 16.4 %collective-permute-start.23 = (f32[128,2,128]{0,2,1:T(8,128)S(1)}, f32[128,2,128]{0,2,1:T(8,128)S(1)}, u32[]{:S(2)}, u32[]{:S(2)}) collective-permute-start(f32[128,2,128]{0,2,1:T(8,128)S(1)} %get-tuple-element.1337), channel_id=1, source_target_pairs={{0,16},{4,20},{8,24},{12,28},{16,32},{20,36},{24,40},{28,44},{32,4... | collective-permute-start | bytes 393224 | tf_op jit(solution)/shard_map/ppermute | solution.py:35
  117.6 16.9 %collective-permute-start.27 = (f32[128,2,128]{0,2,1:T(8,128)S(1)}, f32[128,2,128]{0,2,1:T(8,128)S(1)}, u32[]{:S(2)}, u32[]{:S(2)}) collective-permute-start(f32[128,2,128]{0,2,1:T(8,128)S(1)} %get-tuple-element.1349), channel_id=1, source_target_pairs={{16,0},{20,4},{24,8},{28,12},{32,16},{36,20},{40,24},{44,28},{48,3... | collective-permute-start | bytes 393224 | tf_op jit(solution)/shard_map/ppermute | solution.py:35
  184.1 17.9 %collective-permute-start.35 = (f32[128,2,128]{0,2,1:T(8,128)S(1)}, f32[128,2,128]{0,2,1:T(8,128)S(1)}, u32[]{:S(2)}, u32[]{:S(2)}) collective-permute-start(f32[128,2,128]{0,2,1:T(8,128)S(1)} %get-tuple-element.1325), channel_id=1, source_target_pairs={{16,0},{20,4},{24,8},{28,12},{32,16},{36,20},{40,24},{44,28},{48,3... | collective-permute-start | bytes 393224 | tf_op jit(solution)/shard_map/ppermute | solution.py:35
  186.2 20.0 %collective-permute-start.36 = (f32[128,2,128]{0,2,1:T(8,128)S(1)}, f32[128,2,128]{0,2,1:T(8,128)S(1)}, u32[]{:S(2)}, u32[]{:S(2)}) collective-permute-start(f32[128,2,128]{0,2,1:T(8,128)S(1)} %get-tuple-element.1324), channel_id=1, source_target_pairs={{0,4},{4,8},{8,12},{12,16},{16,20},{20,24},{24,28},{28,32},{32,36}... | collective-permute-start | bytes 393224 | tf_op jit(solution)/shard_map/ppermute | solution.py:35
  188.6 19.8 %collective-permute-start.37 = (f32[128,2,128]{0,2,1:T(8,128)S(1)}, f32[128,2,128]{0,2,1:T(8,128)S(1)}, u32[]{:S(2)}, u32[]{:S(2)}) collective-permute-start(f32[128,2,128]{0,2,1:T(8,128)S(1)} %get-tuple-element.1323), channel_id=1, source_target_pairs={{0,8},{4,12},{8,16},{12,20},{16,24},{20,28},{24,32},{28,36},{32,40... | collective-permute-start | bytes 393224 | tf_op jit(solution)/shard_map/ppermute | solution.py:35
  192.0 18.7 %collective-permute-start.38 = (f32[128,2,128]{0,2,1:T(8,128)S(1)}, f32[128,2,128]{0,2,1:T(8,128)S(1)}, u32[]{:S(2)}, u32[]{:S(2)}) collective-permute-start(f32[128,2,128]{0,2,1:T(8,128)S(1)} %get-tuple-element.1322), channel_id=1, source_target_pairs={{0,12},{4,16},{8,20},{12,24},{16,28},{20,32},{24,36},{28,40},{32,4... | collective-permute-start | bytes 393224 | tf_op jit(solution)/shard_map/ppermute | solution.py:35
  196.6 16.5 %collective-permute-start.39 = (f32[128,2,128]{0,2,1:T(8,128)S(1)}, f32[128,2,128]{0,2,1:T(8,128)S(1)}, u32[]{:S(2)}, u32[]{:S(2)}) collective-permute-start(f32[128,2,128]{0,2,1:T(8,128)S(1)} %get-tuple-element.1321), channel_id=1, source_target_pairs={{0,16},{4,20},{8,24},{12,28},{16,32},{20,36},{24,40},{28,44},{32,4... | collective-permute-start | bytes 393224 | tf_op jit(solution)/shard_map/ppermute | solution.py:35
  210.7 16.9 %collective-permute-start.43 = (f32[128,2,128]{0,2,1:T(8,128)S(1)}, f32[128,2,128]{0,2,1:T(8,128)S(1)}, u32[]{:S(2)}, u32[]{:S(2)}) collective-permute-start(f32[128,2,128]{0,2,1:T(8,128)S(1)} %get-tuple-element.1333), channel_id=1, source_target_pairs={{16,0},{20,4},{24,8},{28,12},{32,16},{36,20},{40,24},{44,28},{48,3... | collective-permute-start | bytes 393224 | tf_op jit(solution)/shard_map/ppermute | solution.py:35
  274.0 18.0 %collective-permute-start.51 = (f32[128,2,128]{0,2,1:T(8,128)S(1)}, f32[128,2,128]{0,2,1:T(8,128)S(1)}, u32[]{:S(2)}, u32[]{:S(2)}) collective-permute-start(f32[128,2,128]{0,2,1:T(8,128)S(1)} %get-tuple-element.1309), channel_id=1, source_target_pairs={{16,0},{20,4},{24,8},{28,12},{32,16},{36,20},{40,24},{44,28},{48,3... | collective-permute-start | bytes 393224 | tf_op jit(solution)/shard_map/ppermute | solution.py:35
  275.9 20.1 %collective-permute-start.52 = (f32[128,2,128]{0,2,1:T(8,128)S(1)}, f32[128,2,128]{0,2,1:T(8,128)S(1)}, u32[]{:S(2)}, u32[]{:S(2)}) collective-permute-start(f32[128,2,128]{0,2,1:T(8,128)S(1)} %get-tuple-element.1308), channel_id=1, source_target_pairs={{0,4},{4,8},{8,12},{12,16},{16,20},{20,24},{24,28},{28,32},{32,36}... | collective-permute-start | bytes 393224 | tf_op jit(solution)/shard_map/ppermute | solution.py:35
  278.4 19.9 %collective-permute-start.53 = (f32[128,2,128]{0,2,1:T(8,128)S(1)}, f32[128,2,128]{0,2,1:T(8,128)S(1)}, u32[]{:S(2)}, u32[]{:S(2)}) collective-permute-start(f32[128,2,128]{0,2,1:T(8,128)S(1)} %get-tuple-element.1307), channel_id=1, source_target_pairs={{0,8},{4,12},{8,16},{12,20},{16,24},{20,28},{24,32},{28,36},{32,40... | collective-permute-start | bytes 393224 | tf_op jit(solution)/shard_map/ppermute | solution.py:35
  281.8 18.8 %collective-permute-start.54 = (f32[128,2,128]{0,2,1:T(8,128)S(1)}, f32[128,2,128]{0,2,1:T(8,128)S(1)}, u32[]{:S(2)}, u32[]{:S(2)}) collective-permute-start(f32[128,2,128]{0,2,1:T(8,128)S(1)} %get-tuple-element.1306), channel_id=1, source_target_pairs={{0,12},{4,16},{8,20},{12,24},{16,28},{20,32},{24,36},{28,40},{32,4... | collective-permute-start | bytes 393224 | tf_op jit(solution)/shard_map/ppermute | solution.py:35
  300.6 16.9 %collective-permute-start.59 = (f32[128,2,128]{0,2,1:T(8,128)S(1)}, f32[128,2,128]{0,2,1:T(8,128)S(1)}, u32[]{:S(2)}, u32[]{:S(2)}) collective-permute-start(f32[128,2,128]{0,2,1:T(8,128)S(1)} %get-tuple-element.1317), channel_id=1, source_target_pairs={{16,0},{20,4},{24,8},{28,12},{32,16},{36,20},{40,24},{44,28},{48,3... | collective-permute-start | bytes 393224 | tf_op jit(solution)/shard_map/ppermute | solution.py:35
  364.0 18.0 %collective-permute-start.67 = (f32[128,2,128]{0,2,1:T(8,128)S(1)}, f32[128,2,128]{0,2,1:T(8,128)S(1)}, u32[]{:S(2)}, u32[]{:S(2)}) collective-permute-start(f32[128,2,128]{0,2,1:T(8,128)S(1)} %get-tuple-element.1293), channel_id=1, source_target_pairs={{16,0},{20,4},{24,8},{28,12},{32,16},{36,20},{40,24},{44,28},{48,3... | collective-permute-start | bytes 393224 | tf_op jit(solution)/shard_map/ppermute | solution.py:35
  366.0 20.1 %collective-permute-start.68 = (f32[128,2,128]{0,2,1:T(8,128)S(1)}, f32[128,2,128]{0,2,1:T(8,128)S(1)}, u32[]{:S(2)}, u32[]{:S(2)}) collective-permute-start(f32[128,2,128]{0,2,1:T(8,128)S(1)} %get-tuple-element.1292), channel_id=1, source_target_pairs={{0,4},{4,8},{8,12},{12,16},{16,20},{20,24},{24,28},{28,32},{32,36}... | collective-permute-start | bytes 393224 | tf_op jit(solution)/shard_map/ppermute | solution.py:35
  368.4 19.9 %collective-permute-start.69 = (f32[128,2,128]{0,2,1:T(8,128)S(1)}, f32[128,2,128]{0,2,1:T(8,128)S(1)}, u32[]{:S(2)}, u32[]{:S(2)}) collective-permute-start(f32[128,2,128]{0,2,1:T(8,128)S(1)} %get-tuple-element.1291), channel_id=1, source_target_pairs={{0,8},{4,12},{8,16},{12,20},{16,24},{20,28},{24,32},{28,36},{32,40... | collective-permute-start | bytes 393224 | tf_op jit(solution)/shard_map/ppermute | solution.py:35
  371.8 18.8 %collective-permute-start.70 = (f32[128,2,128]{0,2,1:T(8,128)S(1)}, f32[128,2,128]{0,2,1:T(8,128)S(1)}, u32[]{:S(2)}, u32[]{:S(2)}) collective-permute-start(f32[128,2,128]{0,2,1:T(8,128)S(1)} %get-tuple-element.1290), channel_id=1, source_target_pairs={{0,12},{4,16},{8,20},{12,24},{16,28},{20,32},{24,36},{28,40},{32,4... | collective-permute-start | bytes 393224 | tf_op jit(solution)/shard_map/ppermute | solution.py:35
  390.6 16.9 %collective-permute-start.75 = (f32[128,2,128]{0,2,1:T(8,128)S(1)}, f32[128,2,128]{0,2,1:T(8,128)S(1)}, u32[]{:S(2)}, u32[]{:S(2)}) collective-permute-start(f32[128,2,128]{0,2,1:T(8,128)S(1)} %get-tuple-element.1301), channel_id=1, source_target_pairs={{16,0},{20,4},{24,8},{28,12},{32,16},{36,20},{40,24},{44,28},{48,3... | collective-permute-start | bytes 393224 | tf_op jit(solution)/shard_map/ppermute | solution.py:35
  (65 other events, 951.8 us)
